TPU v7x, 512 devices: a whole 4x8x8 slice. The times are simulated.
512 devices in a mesh: pair: 32 (over y_lo, z), day: 16 (over y_hi, x, core).
Axes of the slice: x: 4, y: 8 (y_hi: 2, y_lo: 4; y = y_hi * 4 + y_lo), z: 8, core: 2. Of those that a mesh axis runs over, the one named last changes fastest.
Arguments:
- spectra: bfloat16 [32, 2, 2048, 1024], P('day', None, 'pair'), may hold values from -6 to 6
- band_weights: float32 [8, 2048], replicated, may hold values from 0.05 to 1
- pair_stations: int32 [1536, 2], replicated, may hold values from 0 to 1023
- block_live: int32 [512], P(('pair', 'day')), may hold values from 1 to 3, 1152 in all
- windows: int32 [1536, 8, 2], P(('pair', 'day')), may hold values from 0 to 4096, as said below
- observed: bfloat16 [1536, 8, 4096], P(('pair', 'day')), may hold values from -6 to 6
Outputs:
- adjoint: float32 [32, 2, 2048, 1024], P('day', None, 'pair')
Inputs may be any that keep to these rules, and one draw needn't show every extreme that they name: Block b holds pairs b * 3 to b * 3 + 2, and its first block_live[b] pairs are live. windows[p, k, 0] < windows[p, k, 1].
All inputs are finite; a program needn't handle non-finite values.
Results may differ from a plain program's by a relative error of at most 0.0035.
Values sent between devices are 32-bit elements; how exact they have to be, the bound alone decides.
A program may use at most 64 MiB of HBM per device.

v0:
```python
import math

import jax
import jax.numpy as jnp
from jax import lax
from jax.sharding import PartitionSpec as P


def table_block(start, width, lags):
    half = lags // 2
    freqs = jnp.arange(half, dtype=jnp.int32)
    lag_index = start + jnp.arange(width, dtype=jnp.int32)
    phase = freqs[:, None] * lag_index[None, :] % lags
    angle = phase.astype(jnp.float32) * (2.0 * math.pi / lags)
    return jnp.concatenate([jnp.cos(angle), -jnp.sin(angle)], axis=0).astype(jnp.bfloat16)


def one_hot_rows(identity, columns):
    return (identity[:, None] == columns[None, :]).astype(jnp.bfloat16)


def gather_rows(flat_spectra, stations):
    count = stations.shape[0]
    station_count = flat_spectra.shape[1]
    width = math.gcd(count, 512)
    columns = jnp.arange(station_count, dtype=jnp.int32)
    dims = (((1,), (1,)), ((), ()))

    def gather_step(index, buffers):
        start = index * width
        identity = lax.dynamic_slice_in_dim(stations, start, width, 0)
        first_hot = one_hot_rows(identity[:, 0], columns)
        second_hot = one_hot_rows(identity[:, 1], columns)
        first_part = lax.dot_general(
            flat_spectra, first_hot, dims, preferred_element_type=jnp.float32
        ).astype(jnp.bfloat16)
        second_part = lax.dot_general(
            flat_spectra, second_hot, dims, preferred_element_type=jnp.float32
        ).astype(jnp.bfloat16)
        return (
            lax.dynamic_update_slice_in_dim(buffers[0], first_part, start, 1),
            lax.dynamic_update_slice_in_dim(buffers[1], second_part, start, 1),
        )

    empty = jnp.zeros((flat_spectra.shape[0], count), jnp.bfloat16)
    return lax.fori_loop(0, count // width, gather_step, (empty, empty))


def cross_stack(first_rows, second_rows, day_count, freq_count):
    count = first_rows.shape[1]
    first = first_rows.reshape(day_count, 2, freq_count, count).astype(jnp.float32)
    second = second_rows.reshape(day_count, 2, freq_count, count).astype(jnp.float32)
    real_part = jnp.sum(first[:, 0] * second[:, 0] + first[:, 1] * second[:, 1], axis=0)
    imag_part = jnp.sum(first[:, 0] * second[:, 1] - first[:, 1] * second[:, 0], axis=0)
    return jnp.stack([real_part, imag_part]).transpose(0, 2, 1)


def add_to_stations(accum, to_first, to_second, stations):
    count = stations.shape[0]
    station_count = accum.shape[1]
    width = math.gcd(count, 512)
    columns = jnp.arange(station_count, dtype=jnp.int32)

    def add_step(index, total):
        start = index * width
        identity = lax.dynamic_slice_in_dim(stations, start, width, 0)
        hot = jnp.concatenate(
            [one_hot_rows(identity[:, 0], columns), one_hot_rows(identity[:, 1], columns)], axis=0
        )
        terms = jnp.concatenate(
            [
                lax.dynamic_slice_in_dim(to_first, start, width, 1),
                lax.dynamic_slice_in_dim(to_second, start, width, 1),
            ],
            axis=1,
        )
        return total + jnp.dot(
            terms,
            hot.astype(jnp.float32),
            precision=lax.Precision.HIGHEST,
            preferred_element_type=jnp.float32,
        )

    return lax.fori_loop(0, count // width, add_step, accum)


def station_terms(accum, first_rows, second_rows, grads, stations, day_count):
    count = first_rows.shape[1]
    freq_count = grads.shape[2]
    first = first_rows.reshape(day_count, 2, freq_count, count).astype(jnp.float32)
    second = second_rows.reshape(day_count, 2, freq_count, count).astype(jnp.float32)
    turned = grads.transpose(0, 2, 1)
    grad_real = turned[0][None]
    grad_imag = turned[1][None]
    to_first = jnp.stack(
        [
            grad_real * second[:, 0] + grad_imag * second[:, 1],
            grad_real * second[:, 1] - grad_imag * second[:, 0],
        ],
        axis=1,
    ).reshape(-1, count)
    to_second = jnp.stack(
        [
            grad_real * first[:, 0] - grad_imag * first[:, 1],
            grad_real * first[:, 1] + grad_imag * first[:, 0],
        ],
        axis=1,
    ).reshape(-1, count)
    return add_to_stations(accum, to_first, to_second, stations)


def body(spectra, band_weights, pair_stations, block_live, windows, observed):
    n_pair = lax.axis_size("pair")
    n_day = lax.axis_size("day")
    per_block, bands, lags = observed.shape
    half = lags // 2
    day_count = spectra.shape[0]
    freq_count = spectra.shape[2]
    station_count = spectra.shape[3]
    days = day_count * n_day
    ordered = (
        pair_stations.reshape(n_pair, n_day, per_block, 2).transpose(1, 0, 2, 3).reshape(-1, 2)
    )
    flat_spectra = spectra.reshape(-1, station_count)
    first_rows, second_rows = gather_rows(flat_spectra, ordered)
    local_stack = cross_stack(first_rows, second_rows, day_count, freq_count)
    total = lax.psum(local_stack, "day")
    day_share = lax.dynamic_slice_in_dim(
        total, lax.axis_index("day") * (n_pair * per_block), n_pair * per_block, 1
    )
    pair_stack = lax.all_to_all(day_share, "pair", split_axis=1, concat_axis=2, tiled=True)
    weights_full = jnp.concatenate([band_weights, band_weights], axis=1)
    flat_stack = jnp.concatenate([pair_stack[0], pair_stack[1]], axis=1)
    weighted = (
        (flat_stack[:, None, :] * weights_full[None])
        .astype(jnp.bfloat16)
        .reshape(per_block * bands, lags)
    )
    live = jnp.arange(per_block, dtype=jnp.int32) < block_live[0]
    row_live = jnp.repeat(live, bands)
    lower_lag = windows[:, :, 0].reshape(-1)
    upper_lag = windows[:, :, 1].reshape(-1)
    observed_rows = observed.reshape(per_block * bands, lags)
    width = min(256, lags)
    forward_scale = 2.0 / math.sqrt(lags * days)
    adjoint_scale = 1.0 / math.sqrt(lags)

    def lag_step(index, accum):
        start = index * width
        block_table = table_block(start, width, lags)
        corr = forward_scale * jnp.dot(weighted, block_table, preferred_element_type=jnp.float32)
        lag_index = start + jnp.arange(width, dtype=jnp.int32)
        inside = (
            row_live[:, None]
            & (lag_index[None, :] >= lower_lag[:, None])
            & (lag_index[None, :] < upper_lag[:, None])
        )
        target = lax.dynamic_slice_in_dim(observed_rows, start, width, 1).astype(jnp.float32)
        misfit = jnp.where(inside, corr - target, 0.0).astype(jnp.bfloat16)
        return accum + lax.dot_general(
            misfit, block_table, (((1,), (1,)), ((), ())), preferred_element_type=jnp.float32
        )

    adjoint_rows = lax.fori_loop(
        0, lags // width, lag_step, jnp.zeros((per_block * bands, lags), jnp.float32)
    )
    summed = jnp.sum(adjoint_rows.reshape(per_block, bands, lags) * weights_full[None], axis=1)
    adjoint_spec = adjoint_scale * summed
    adjoint_split = adjoint_spec.reshape(per_block, 2, half).transpose(1, 0, 2)
    spread = lax.all_to_all(adjoint_split, "pair", split_axis=2, concat_axis=1, tiled=True)
    start_total = jnp.zeros((flat_spectra.shape[0], station_count), jnp.float32)
    all_pairs = lax.all_gather(spread, "day", axis=1, tiled=True)
    flat_out = station_terms(start_total, first_rows, second_rows, all_pairs, ordered, day_count)
    return flat_out.reshape(spectra.shape)


def solution(mesh):
    in_specs = (
        P("day", None, "pair", None),
        P(),
        P(),
        P(("pair", "day")),
        P(("pair", "day"), None, None),
        P(("pair", "day"), None, None),
    )
    out_specs = P("day", None, "pair", None)
    return jax.shard_map(body, mesh=mesh, in_specs=in_specs, out_specs=out_specs, check_vma=False)
```

profile of v0, /device:TPU:1, one launch (start us, length us, event | category | flops | bytes accessed | tf_op | source)
XLA Modules:
  0.0 495.4 jit_solution(16453960934737975883)
XLA Ops:
  8.3 4.5 while.49
  16.7 188.6 %all-reduce.2.cloned.1.call-done = f32[2,1536,64]{1,2,0:T(8,128)} async-done(((f32[2,1536,64]{1,2,0:T(8,128)}), f32[2,1536,64]{1,2,0:T(8,128)}) %all-reduce.2.cloned.1.call-update) | async-done | bytes 786448 | tf_op jit(solution)/shard_map/psum | solution.py:127
  207.2 7.7 %all-to-all-start = ((f32[32,1,384]{2,1,0:T(1,128)}), f32[32,1,384]{2,1,0:T(1,128)S(1)}, u32[]{:S(2)}, u32[]{:S(2)}) async-start(f32[32,1,384]{2,1,0:T(1,128)} %reshape.72), calls=%async_computation | async-start | bytes 98304 | tf_op jit(solution)/shard_map/all_to_all | solution.py:131
  214.9 9.1 %all-to-all-done = f32[32,1,384]{2,1,0:T(1,128)S(1)} async-done(((f32[32,1,384]{2,1,0:T(1,128)}), f32[32,1,384]{2,1,0:T(1,128)S(1)}, u32[]{:S(2)}, u32[]{:S(2)}) %all-to-all-start) | async-done | bytes 49184 | tf_op jit(solution)/shard_map/all_to_all | solution.py:131
  225.7 176.8 %while.51 = (s32[]{:T(128)}, f32[24,4096]{1,0:T(8,128)S(1)}, s32[3,8,1]{1,0,2:T(4,128)}, s32[3,8,1]{1,0,2:T(4,128)}, bf16[24,4096]{1,0:T(8,128)(2,1)}, /*index=5...) while((s32[]{:T(128)}, f32[24,4096]{1,0:T(8,128)S(1)}, ...), condition=%wide.wide.region_6.7_spmd.clone, body=%wide.wide.region_5.6_spmd.clone.sunk | while | flops 118413576 | bytes 7291664 | solution.py:164
  225.8 8.6 %cosine_convert_fusion.3 = (bf16[2048,256]{1,0:T(8,128)(2,1)S(1)}, bf16[2048,256]{1,0:T(8,128)(2,1)S(1)}) fusion(s32[256]{0:T(256)S(1)} %iota_add_fusion.3), kind=kLoop, calls=%fused_computation.26.clone.clone.1 | loop fusion | flops 8912896 | bytes 2098176 | tf_op jit(solution)/shard_map/convert.1
  236.8 8.6 %cosine_convert_fusion.3 = (bf16[2048,256]{1,0:T(8,128)(2,1)S(1)}, bf16[2048,256]{1,0:T(8,128)(2,1)S(1)}) fusion(s32[256]{0:T(256)S(1)} %iota_add_fusion.3), kind=kLoop, calls=%fused_computation.26.clone.clone.1 | loop fusion | flops 8912896 | bytes 2098176 | tf_op jit(solution)/shard_map/convert.1
  247.9 8.6 %cosine_convert_fusion.3 = (bf16[2048,256]{1,0:T(8,128)(2,1)S(1)}, bf16[2048,256]{1,0:T(8,128)(2,1)S(1)}) fusion(s32[256]{0:T(256)S(1)} %iota_add_fusion.3), kind=kLoop, calls=%fused_computation.26.clone.clone.1 | loop fusion | flops 8912896 | bytes 2098176 | tf_op jit(solution)/shard_map/convert.1
  258.9 8.6 %cosine_convert_fusion.3 = (bf16[2048,256]{1,0:T(8,128)(2,1)S(1)}, bf16[2048,256]{1,0:T(8,128)(2,1)S(1)}) fusion(s32[256]{0:T(256)S(1)} %iota_add_fusion.3), kind=kLoop, calls=%fused_computation.26.clone.clone.1 | loop fusion | flops 8912896 | bytes 2098176 | tf_op jit(solution)/shard_map/convert.1
  270.0 8.6 %cosine_convert_fusion.3 = (bf16[2048,256]{1,0:T(8,128)(2,1)S(1)}, bf16[2048,256]{1,0:T(8,128)(2,1)S(1)}) fusion(s32[256]{0:T(256)S(1)} %iota_add_fusion.3), kind=kLoop, calls=%fused_computation.26.clone.clone.1 | loop fusion | flops 8912896 | bytes 2098176 | tf_op jit(solution)/shard_map/convert.1
  281.0 8.6 %cosine_convert_fusion.3 = (bf16[2048,256]{1,0:T(8,128)(2,1)S(1)}, bf16[2048,256]{1,0:T(8,128)(2,1)S(1)}) fusion(s32[256]{0:T(256)S(1)} %iota_add_fusion.3), kind=kLoop, calls=%fused_computation.26.clone.clone.1 | loop fusion | flops 8912896 | bytes 2098176 | tf_op jit(solution)/shard_map/convert.1
  292.1 8.6 %cosine_convert_fusion.3 = (bf16[2048,256]{1,0:T(8,128)(2,1)S(1)}, bf16[2048,256]{1,0:T(8,128)(2,1)S(1)}) fusion(s32[256]{0:T(256)S(1)} %iota_add_fusion.3), kind=kLoop, calls=%fused_computation.26.clone.clone.1 | loop fusion | flops 8912896 | bytes 2098176 | tf_op jit(solution)/shard_map/convert.1
  303.1 8.6 %cosine_convert_fusion.3 = (bf16[2048,256]{1,0:T(8,128)(2,1)S(1)}, bf16[2048,256]{1,0:T(8,128)(2,1)S(1)}) fusion(s32[256]{0:T(256)S(1)} %iota_add_fusion.3), kind=kLoop, calls=%fused_computation.26.clone.clone.1 | loop fusion | flops 8912896 | bytes 2098176 | tf_op jit(solution)/shard_map/convert.1
  314.2 8.6 %cosine_convert_fusion.3 = (bf16[2048,256]{1,0:T(8,128)(2,1)S(1)}, bf16[2048,256]{1,0:T(8,128)(2,1)S(1)}) fusion(s32[256]{0:T(256)S(1)} %iota_add_fusion.3), kind=kLoop, calls=%fused_computation.26.clone.clone.1 | loop fusion | flops 8912896 | bytes 2098176 | tf_op jit(solution)/shard_map/convert.1
  325.2 8.6 %cosine_convert_fusion.3 = (bf16[2048,256]{1,0:T(8,128)(2,1)S(1)}, bf16[2048,256]{1,0:T(8,128)(2,1)S(1)}) fusion(s32[256]{0:T(256)S(1)} %iota_add_fusion.3), kind=kLoop, calls=%fused_computation.26.clone.clone.1 | loop fusion | flops 8912896 | bytes 2098176 | tf_op jit(solution)/shard_map/convert.1
  336.3 8.6 %cosine_convert_fusion.3 = (bf16[2048,256]{1,0:T(8,128)(2,1)S(1)}, bf16[2048,256]{1,0:T(8,128)(2,1)S(1)}) fusion(s32[256]{0:T(256)S(1)} %iota_add_fusion.3), kind=kLoop, calls=%fused_computation.26.clone.clone.1 | loop fusion | flops 8912896 | bytes 2098176 | tf_op jit(solution)/shard_map/convert.1
  347.3 8.6 %cosine_convert_fusion.3 = (bf16[2048,256]{1,0:T(8,128)(2,1)S(1)}, bf16[2048,256]{1,0:T(8,128)(2,1)S(1)}) fusion(s32[256]{0:T(256)S(1)} %iota_add_fusion.3), kind=kLoop, calls=%fused_computation.26.clone.clone.1 | loop fusion | flops 8912896 | bytes 2098176 | tf_op jit(solution)/shard_map/convert.1
  358.4 8.6 %cosine_convert_fusion.3 = (bf16[2048,256]{1,0:T(8,128)(2,1)S(1)}, bf16[2048,256]{1,0:T(8,128)(2,1)S(1)}) fusion(s32[256]{0:T(256)S(1)} %iota_add_fusion.3), kind=kLoop, calls=%fused_computation.26.clone.clone.1 | loop fusion | flops 8912896 | bytes 2098176 | tf_op jit(solution)/shard_map/convert.1
  369.4 8.6 %cosine_convert_fusion.3 = (bf16[2048,256]{1,0:T(8,128)(2,1)S(1)}, bf16[2048,256]{1,0:T(8,128)(2,1)S(1)}) fusion(s32[256]{0:T(256)S(1)} %iota_add_fusion.3), kind=kLoop, calls=%fused_computation.26.clone.clone.1 | loop fusion | flops 8912896 | bytes 2098176 | tf_op jit(solution)/shard_map/convert.1
  380.5 8.6 %cosine_convert_fusion.3 = (bf16[2048,256]{1,0:T(8,128)(2,1)S(1)}, bf16[2048,256]{1,0:T(8,128)(2,1)S(1)}) fusion(s32[256]{0:T(256)S(1)} %iota_add_fusion.3), kind=kLoop, calls=%fused_computation.26.clone.clone.1 | loop fusion | flops 8912896 | bytes 2098176 | tf_op jit(solution)/shard_map/convert.1
  391.5 8.6 %cosine_convert_fusion.3 = (bf16[2048,256]{1,0:T(8,128)(2,1)S(1)}, bf16[2048,256]{1,0:T(8,128)(2,1)S(1)}) fusion(s32[256]{0:T(256)S(1)} %iota_add_fusion.3), kind=kLoop, calls=%fused_computation.26.clone.clone.1 | loop fusion | flops 8912896 | bytes 2098176 | tf_op jit(solution)/shard_map/convert.1
  411.4 9.1 %all-to-all-done.1 = f32[32,1,384]{2,1,0:T(1,128)S(1)} async-done(((f32[32,1,384]{2,1,0:T(1,128)}), f32[32,1,384]{2,1,0:T(1,128)S(1)}, u32[]{:S(2)}, u32[]{:S(2)}) %all-to-all-start.1) | async-done | bytes 49184 | tf_op jit(solution)/shard_map/all_to_all | solution.py:170
  425.5 39.5 %all_gather.3 = f32[2,1536,64]{2,0,1:T(2,128)S(1)} all-gather(f32[2,96,64]{2,0,1:T(2,128)S(1)} %bitcast.109), channel_id=1, replica_groups=mesh['pair'=32,'day'=16] {'day'}, dimensions={1}, use_global_device_ids=true | all-gather | bytes 835584 | tf_op jit(solution)/shard_map/all_gather | solution.py:172
  475.0 12.5 %while.50 = (s32[]{:T(128)}, f32[256,1024]{1,0:T(8,128)S(1)}, f32[256,1536]{1,0:T(8,128)}, f32[256,1536]{1,0:T(8,128)}, s32[1536,2]{0,1:T(2,128)S(1)}, /*index=5...) while((s32[]{:T(128)}, f32[256,1024]{1,0:T(8,128)S(1)}, f32[256,1536]{1,0:T(8,128)}, ...), condition=%wide.region_9.10_spmd.clone.clone, body=%wide.region_8.9_spmd.clone.clone.sunk | while | flops 3224109056 | bytes 7352501 | solution.py:84
  (164 shorter events, 88.3 us)
Async XLA Ops:
  6.5 1.8 copy-start.8
  6.5 198.8 %all-reduce.2.cloned.1.call-start = ((), (), s32[]{:S(2)}) async-start(), calls=%async_computation.2 | async-start | bytes 1572864 | tf_op jit(solution)/shard_map/psum | solution.py:127
  13.2 1.1 copy-start
  13.2 1.6 copy-start.2
  14.8 1.0 copy-start.7
  14.8 1.8 copy-start.4
  15.8 209.9 %copy-start.5 = (s32[3,8,1]{1,0,2:T(4,128)}, s32[3,8,1]{1,0,2:T(4,128)S(1)}, u32[]{:S(2)}) copy-start(s32[3,8,1]{1,0,2:T(4,128)S(1)} %copy.75) | copy-start | bytes 292
  15.9 209.8 %copy-start.6 = (s32[3,8,1]{1,0,2:T(4,128)}, s32[3,8,1]{1,0,2:T(4,128)S(1)}, u32[]{:S(2)}) copy-start(s32[3,8,1]{1,0,2:T(4,128)S(1)} %copy.76) | copy-start | bytes 292
  207.2 16.8 %all-to-all-start = ((f32[32,1,384]{2,1,0:T(1,128)}), f32[32,1,384]{2,1,0:T(1,128)S(1)}, u32[]{:S(2)}, u32[]{:S(2)}) async-start(f32[32,1,384]{2,1,0:T(1,128)} %reshape.72), calls=%async_computation | async-start | bytes 98304 | tf_op jit(solution)/shard_map/all_to_all | solution.py:131
  407.5 13.0 %all-to-all-start.1 = ((f32[32,1,384]{2,1,0:T(1,128)}), f32[32,1,384]{2,1,0:T(1,128)S(1)}, u32[]{:S(2)}, u32[]{:S(2)}) async-start(f32[32,1,384]{2,1,0:T(1,128)} %reshape.74), calls=%async_computation.1 | async-start | bytes 98304 | tf_op jit(solution)/shard_map/all_to_all | solution.py:170
  464.9 5.7 %copy-start.1 = (f32[2,2,64,1536]{3,2,1,0:T(8,128)S(1)}, f32[2,2,64,1536]{3,2,1,0:T(8,128)}, u32[]{:S(2)}) copy-start(f32[2,2,64,1536]{3,2,1,0:T(8,128)} %copy-done) | copy-start | bytes 4718596
  464.9 5.7 %copy-start.3 = (f32[2,2,64,1536]{3,2,1,0:T(8,128)S(1)}, f32[2,2,64,1536]{3,2,1,0:T(8,128)}, u32[]{:S(2)}) copy-start(f32[2,2,64,1536]{3,2,1,0:T(8,128)} %copy-done.2) | copy-start | bytes 4718596
  473.3 1.7 copy-start.9
  487.6 1.0 copy-start.10
Sparse Core Ops, SparseCore 0:
  15.9 189.3 all-reduce.1
where the time goes:
time: 497 us; the launch traced here: 495 us
  waiting for transfers between devices  207 us (42%)
  other arithmetic  148 us (30%)
  matrix products  45 us (9%)
  blocking collectives  39.5 us (8%)
  local copies, waits for them, and re-layouts  29.9 us (6%)
  between operations  14.4 us (3%)
  starting transfers between devices  11.5 us (2%)
    psum x1, waiting for transfers between devices, body(): total = lax.psum(local_stack, 'day')  189 us
    another operation x16, other arithmetic  138 us
    all_gather x1, blocking collectives, body(): all_pairs = lax.all_gather(spread, 'day', axis=1, tiled=True)  39.5 us
    dot_general x16, matrix products, lag_step(): lax.dot_general(misfit, block_table, (((1,), (1,)), ((), ())), preferred_...  35.5 us
    unnamed x29, local copies, waits for them, and re-layouts  10.3 us
  transfers between devices with their start and end apart: 3, of which 3 were waited for; matrix products, arithmetic and copies ran while one was open for 0% of the time, Pallas kernels for 0%

commit v1 on v0

v1 whole, which is shorter than its diff:
```python
import functools
import math

import jax
import jax.numpy as jnp
import numpy as np
from jax import lax
from jax.experimental import pallas as pl
from jax.experimental.pallas import tpu as pltpu
from jax.sharding import PartitionSpec as P

F32 = jnp.float32
BF16 = jnp.bfloat16
MESH = pl.DeviceIdType.MESH
FINE = 32


def split_const(table):
    high = table.astype(jnp.bfloat16)
    low = (table - high.astype(np.float64)).astype(jnp.bfloat16)
    return high, low


@functools.lru_cache(maxsize=None)
def tables(y_lo, n_z):
    count = y_lo * n_z
    coarse = 2 * count
    width = 2 * coarse
    lags = FINE * width
    lanes = 4 * count
    cos_c = np.zeros((4 * lanes, 6 * width))
    t_a = np.arange(width)
    for c in range(2):
        for h in range(2):
            for z in range(n_z):
                for y in range(y_lo):
                    index = 2 * (y * n_z + z) + h
                    angle = 2 * np.pi * ((index * t_a) % width) / width
                    real, imag = (np.cos(angle), np.sin(angle)) if c == 0 else (-np.sin(angle), np.cos(angle))
                    for q in range(3):
                        row = (c * 2 + h) * lanes + (z * 4 + q) * y_lo + y
                        cos_c[row, (2 * q) * width : (2 * q + 1) * width] = real
                        cos_c[row, (2 * q + 1) * width : (2 * q + 2) * width] = imag
    outer_high, outer_low = split_const(cos_c)
    back_high, back_low = split_const(np.ascontiguousarray(cos_c.T))
    fine = np.arange(FINE)
    angle = 2 * np.pi * ((fine[:, None] * fine[None, :]) % FINE) / FINE
    inner = np.concatenate([np.cos(angle), -np.sin(angle)], axis=1)
    inner_tables = np.concatenate(split_const(inner), axis=0)
    inner_back = np.concatenate(split_const(np.ascontiguousarray(inner.T)), axis=0)
    turn = 2 * np.pi * (fine[:, None] * t_a[None, :]) / lags
    twiddle = np.stack([np.cos(turn), np.sin(turn)]).astype(np.float32)
    return outer_high, outer_low, back_high, back_low, inner_tables, inner_back, twiddle


def kernel(dims, days, spec, ids, weights, live, windows, observed, outer_high_hbm, outer_low_hbm, back_high_hbm,
           back_low_hbm, inner, inner_back, twiddle, out, grads, turned, hot, rows, part, sib_in, xs, relay, x_in, y_out,
           y_in, z_out, z_in, z_out2, z_in2, y_out2, obs3, outer_high, outer_low, back_high, back_low, send_sem,
           recv_sem, table_sem):
    y_lo, n_z = dims
    n_y = 2 * y_lo
    chunk = n_y * 24
    half = chunk // 2
    width = 4 * y_lo * n_z
    lanes = width
    lags = FINE * width
    stations = spec.shape[3]
    pair = lax.axis_index("pair")
    day = lax.axis_index("day")
    z = lax.rem(pair, n_z)
    yl = pair // n_z
    yh = day // 8
    x = lax.rem(day // 2, 4)
    core = lax.rem(day, 2)
    y = yh * y_lo + yl

    sibling = {"day": day + 1 - 2 * core}
    right = {"day": yh * 8 + lax.rem(x + 1, 4) * 2 + core}
    left = {"day": yh * 8 + lax.rem(x + 3, 4) * 2 + core}

    def y_device(other):
        return {"pair": lax.rem(other, y_lo) * n_z + z, "day": (other // y_lo) * 8 + x * 2 + core}

    def z_device(other):
        return {"pair": yl * n_z + other}

    barrier = pltpu.get_barrier_semaphore()
    for device in (
        [sibling, right, left]
        + [y_device(lax.rem(y + step, n_y)) for step in range(1, n_y)]
        + [z_device(lax.rem(z + step, n_z)) for step in range(1, n_z)]
    ):
        pl.semaphore_signal(barrier, inc=1, device_id=device, device_id_type=MESH)

    table_copies = []
    for index, (source, target) in enumerate(
        [(outer_high_hbm, outer_high), (outer_low_hbm, outer_low), (back_high_hbm, back_high), (back_low_hbm, back_low)]
    ):
        copy = pltpu.make_async_copy(source, target, table_sem.at[index])
        copy.start()
        table_copies.append(copy)

    sent = []

    def send(source, target, index, device):
        copy = pltpu.make_async_remote_copy(
            src_ref=source,
            dst_ref=target,
            send_sem=send_sem.at[index],
            recv_sem=recv_sem.at[index],
            device_id=device,
            device_id_type=MESH,
        )
        copy.start()
        sent.append(copy)
        return copy

    flat = jnp.concatenate([spec[0, 0], spec[1, 0], spec[0, 1], spec[1, 1]], axis=0)
    turned[...] = flat.astype(F32).T.astype(BF16)
    station_index = lax.broadcasted_iota(jnp.int32, (chunk, stations), 1)
    low_lanes = lax.broadcasted_iota(jnp.int32, (chunk, 128), 1) < 64

    def cross(which, order):
        owner = lax.rem(x + order, 4)
        row = which * 4 + owner
        found = []
        for side in range(2):
            mark = (station_index == ids[row, :, side : side + 1]).astype(F32).astype(BF16)
            hot[side, row] = mark
            value = jnp.dot(mark, turned[...], preferred_element_type=F32)
            rows[side, row] = value.astype(BF16)
            found.append(value)
        first, second = found
        a_re, a_im = first[:, :128], first[:, 128:]
        b_re, b_im = second[:, :128], second[:, 128:]
        real = a_re * b_re + a_im * b_im
        imag = a_re * b_im - a_im * b_re
        real = real + pltpu.roll(real, 64, 1)
        imag = imag + pltpu.roll(imag, 64, 1)
        return jnp.where(low_lanes, real, imag)

    orders = (2, 1, 3, 0)
    sib = []
    first_half, second_half = pl.ds(0, half), pl.ds(half, half)

    def step_cross(step):
        def one(which, carry):
            part[which, step] = cross(jnp.where(which == 0, 1 - core, core), orders[step])
            return carry
        return one

    def summed(step):
        sib[step].wait_recv()
        return part[1, step] + sib_in[step]

    for step in range(4):
        lax.fori_loop(0, 2, step_cross(step), 0)
        if step == 0:
            pl.semaphore_wait(barrier, 3 + (n_y - 1) + (n_z - 1))
        sib.append(send(part.at[0, step], sib_in.at[step], step, sibling))
        if step == 1:
            xs[0] = summed(0)
            relay_right = send(xs.at[0, first_half], relay.at[0], 4, right)
            relay_left = send(xs.at[0, second_half], relay.at[1], 5, left)
        if step == 2:
            xs[1] = summed(1)
            arrive = [send(xs.at[1, second_half], x_in.at[0, second_half], 6, right)]
        if step == 3:
            xs[2] = summed(2)
            arrive.append(send(xs.at[2, first_half], x_in.at[1, first_half], 7, left))
    relay_right.wait_recv()
    xs[1, first_half] = xs[1, first_half] + relay[0]
    arrive.append(send(xs.at[1, first_half], x_in.at[0, first_half], 8, right))
    relay_left.wait_recv()
    xs[2, second_half] = xs[2, second_half] + relay[1]
    arrive.append(send(xs.at[2, second_half], x_in.at[1, second_half], 9, left))
    own = summed(3)

    for q in range(3):
        for t_b in range(FINE):
            obs3[8 * q : 8 * q + 8, t_b, :] = observed[q, :, t_b * width : (t_b + 1) * width].astype(F32)
    z_out[...] = jnp.zeros_like(z_out)

    for copy in arrive:
        copy.wait_recv()
    y_out[...] = (own + x_in[0] + x_in[1]).reshape(n_y, 24, 128)
    far_first = sorted(range(1, n_y), key=lambda step: -min(step, n_y - step))
    base = 10
    copies = []
    for step in far_first:
        other = lax.rem(y + step, n_y)
        copies.append(send(y_out.at[other], y_in.at[y], base + step - 1, y_device(other)))
    y_in[y] = y_out[y]
    base += n_y - 1
    for copy in copies:
        copy.wait_recv()
    for low in range(y_lo):
        total = y_in[low] + y_in[y_lo + low]
        for q in range(3):
            z_out[:, q * y_lo + low, :] = total[8 * q : 8 * q + n_z]
    z_far_first = sorted(range(1, n_z), key=lambda step: -min(step, n_z - step))
    copies = []
    for step in z_far_first:
        other = lax.rem(z + step, n_z)
        copies.append(send(z_out.at[other], z_in.at[z], base + step - 1, z_device(other)))
    z_in[z] = z_out[z]
    base += n_z - 1
    for copy in table_copies:
        copy.wait()
    for copy in copies:
        copy.wait_recv()

    stacked = z_in[...].reshape(lanes, 128).T
    blocks = []
    for c in range(2):
        for h in range(2):
            piece = stacked[(2 * c + h) * FINE : (2 * c + h + 1) * FINE]
            scaled = weights[:, h * FINE : (h + 1) * FINE, :] * piece[None]
            blocks.append(scaled.reshape(8 * FINE, lanes).astype(BF16))
    left_side = jnp.concatenate(blocks, axis=1)
    outer = jnp.dot(left_side, outer_high[...], preferred_element_type=F32) + jnp.dot(
        left_side, outer_low[...], preferred_element_type=F32
    )
    cosine, sine = twiddle[0], twiddle[1]
    columns = []
    for q in range(3):
        real = outer[:, 2 * q * width : (2 * q + 1) * width].reshape(8, FINE, width)
        imag = outer[:, (2 * q + 1) * width : (2 * q + 2) * width].reshape(8, FINE, width)
        new_real = real * cosine[None] - imag * sine[None]
        new_imag = real * sine[None] + imag * cosine[None]
        for k in range(8):
            columns.append(jnp.concatenate([new_real[k], new_imag[k]], axis=0))
    middle = jnp.concatenate(columns, axis=1)
    high = middle.astype(BF16)
    low_part = (middle - high.astype(F32)).astype(BF16)
    product = jnp.dot(inner[...], high, preferred_element_type=F32)
    corr = product[:FINE] + product[FINE:] + jnp.dot(inner[:FINE], low_part, preferred_element_type=F32)
    forward_scale = 2.0 / math.sqrt(lags * days)
    lag_index = lax.broadcasted_iota(jnp.int32, (FINE, width), 0) * width + lax.broadcasted_iota(
        jnp.int32, (FINE, width), 1
    )
    alive = live[0]
    pieces = []
    for q in range(3):
        for k in range(8):
            r = 8 * q + k
            upper = jnp.where(q < alive, windows[q, k, 1], 0)
            inside = (lag_index >= windows[q, k, 0]) & (lag_index < upper)
            gap = forward_scale * corr[:, r * width : (r + 1) * width] - obs3[r]
            pieces.append(jnp.where(inside, gap, 0.0).astype(BF16))
    misfit = jnp.concatenate(pieces, axis=1)
    product = jnp.dot(inner_back[...], misfit, preferred_element_type=F32)
    spread = product[: 2 * FINE] + product[2 * FINE :]
    lines = []
    for k in range(8):
        line = []
        for q in range(3):
            r = 8 * q + k
            real = spread[:FINE, r * width : (r + 1) * width]
            imag = spread[FINE:, r * width : (r + 1) * width]
            line.append(real * cosine + imag * sine)
            line.append(imag * cosine - real * sine)
        lines.append(jnp.concatenate(line, axis=1))
    left_side = jnp.concatenate(lines, axis=0)
    high = left_side.astype(BF16)
    low_part = (left_side - high.astype(F32)).astype(BF16)
    bands = (
        jnp.dot(high, back_high[...], preferred_element_type=F32)
        + jnp.dot(high, back_low[...], preferred_element_type=F32)
        + jnp.dot(low_part, back_high[...], preferred_element_type=F32)
    )
    adjoint_scale = 1.0 / math.sqrt(lags)
    blocks = []
    for c in range(2):
        for h in range(2):
            piece = bands[:, (2 * c + h) * lanes : (2 * c + h + 1) * lanes].reshape(8, FINE, lanes)
            blocks.append(adjoint_scale * jnp.sum(piece * weights[:, h * FINE : (h + 1) * FINE, :], axis=0))
    z_out2[...] = jnp.concatenate(blocks, axis=0).T.reshape(n_z, 4 * y_lo, 128)

    copies = []
    for step in z_far_first:
        other = lax.rem(z + step, n_z)
        copies.append(send(z_out2.at[other], z_in2.at[z], base + step - 1, z_device(other)))
    z_in2[z] = z_out2[z]
    base += n_z - 1
    for copy in copies:
        copy.wait_recv()
    if n_z < 8:
        y_out2[...] = jnp.zeros_like(y_out2)
    for low in range(y_lo):
        for q in range(3):
            y_out2[low, 8 * q : 8 * q + n_z, :] = z_in2[:, q * y_lo + low, :]
    here = core * 4 + x
    copies = []
    for step in far_first:
        other = lax.rem(y + step, n_y)
        copies.append(
            send(y_out2.at[lax.rem(other, y_lo)], grads.at[here, pl.ds(pl.multiple_of(y * 24, 8), 24)], base + step - 1,
                 y_device(other))
        )
    grads[here, pl.ds(pl.multiple_of(y * 24, 8), 24)] = y_out2[yl]
    base += n_y - 1
    for copy in copies:
        copy.wait_recv()

    from_left = core * 4 + lax.rem(x + 3, 4)
    from_right = core * 4 + lax.rem(x + 1, 4)
    across = core * 4 + lax.rem(x + 2, 4)
    go_right = send(grads.at[here], grads.at[here], base, right)
    go_left = send(grads.at[here], grads.at[here], base + 1, left)
    ends = [send(grads.at[here], grads.at[here], base + 4, sibling)]
    go_right.wait_recv()
    pass_right = send(grads.at[from_left, first_half], grads.at[from_left, first_half], base + 2, right)
    go_left.wait_recv()
    pass_left = send(grads.at[from_right, second_half], grads.at[from_right, second_half], base + 3, left)
    ends.append(send(grads.at[from_left], grads.at[from_left], base + 5, sibling))
    ends.append(send(grads.at[from_right], grads.at[from_right], base + 6, sibling))
    pass_right.wait_recv()
    pass_left.wait_recv()
    ends.append(send(grads.at[across], grads.at[across], base + 7, sibling))

    def add(which, order):
        owner = lax.rem(x + order, 4)
        row = which * 4 + owner
        grad = grads[row]
        other = pltpu.roll(grad, 64, 1)
        g_re = jnp.where(low_lanes, grad, other)
        g_im = jnp.where(low_lanes, other, grad)
        first = rows[0, row].astype(F32)
        second = rows[1, row].astype(F32)
        a_re, a_im = first[:, :128], first[:, 128:]
        b_re, b_im = second[:, :128], second[:, 128:]
        to_first = jnp.concatenate([g_re * b_re + g_im * b_im, g_re * b_im - g_im * b_re], axis=1)
        to_second = jnp.concatenate([g_re * a_re - g_im * a_im, g_re * a_im + g_im * a_re], axis=1)
        dims_t = (((1,), (0,)), ((), ()))
        total = lax.dot_general(to_first.T.astype(BF16), hot[0, row], dims_t, preferred_element_type=F32)
        return total + lax.dot_general(to_second.T.astype(BF16), hot[1, row], dims_t, preferred_element_type=F32)

    def put(value, fresh):
        for c in range(2):
            for d in range(2):
                piece = value[c * 128 + d * 64 : c * 128 + d * 64 + 64]
                out[d, c] = piece if fresh else out[d, c] + piece

    put(add(core, 0), True)
    for order in (3, 1, 2):
        put(add(core, order), False)
    for copy in ends:
        copy.wait_recv()

    def add_step(order, carry):
        put(add(1 - core, order), False)
        return carry

    lax.fori_loop(0, 4, add_step, 0)
    for copy in sent:
        copy.wait_send()


def body(y_lo, n_z, spectra, band_weights, pair_stations, block_live, windows, observed):
    n_y = 2 * y_lo
    chunk = n_y * 24
    lanes = 4 * y_lo * n_z
    width = lanes
    stations = spectra.shape[3]
    ids = (
        pair_stations.reshape(y_lo, n_z, 2, 4, 2, 3, 2).transpose(4, 3, 2, 0, 5, 1, 6).reshape(8, n_y, 3, n_z, 2)
    )
    if n_z < 8:
        ids = jnp.pad(ids, ((0, 0), (0, 0), (0, 0), (0, 8 - n_z), (0, 0)), constant_values=-1)
    ids = ids.reshape(8, chunk, 2)
    weights = band_weights.reshape(8, y_lo, n_z, 2, FINE).transpose(0, 3, 4, 2, 1)
    weights = jnp.broadcast_to(weights[:, :, :, :, None, :], (8, 2, FINE, n_z, 4, y_lo)).reshape(8, 2 * FINE, lanes)
    outer_high, outer_low, back_high, back_low, inner, inner_back, twiddle = tables(y_lo, n_z)
    n_sem = 10 + 2 * (n_y - 1) + 2 * (n_z - 1) + 8
    vmem = pl.BlockSpec(memory_space=pltpu.VMEM)
    smem = pl.BlockSpec(memory_space=pltpu.SMEM)
    anywhere = pl.BlockSpec(memory_space=pl.ANY)
    return pl.pallas_call(
        functools.partial(kernel, (y_lo, n_z), 32),
        out_shape=jax.ShapeDtypeStruct(spectra.shape, F32),
        in_specs=[vmem, vmem, vmem, smem, smem, vmem, anywhere, anywhere, anywhere, anywhere, vmem, vmem, vmem],
        out_specs=vmem,
        scratch_shapes=[
            pltpu.VMEM((8, chunk, 128), F32),
            pltpu.VMEM((stations, 256), BF16),
            pltpu.VMEM((2, 8, chunk, stations), BF16),
            pltpu.VMEM((2, 8, chunk, 256), BF16),
            pltpu.VMEM((2, 4, chunk, 128), F32),
            pltpu.VMEM((4, chunk, 128), F32),
            pltpu.VMEM((3, chunk, 128), F32),
            pltpu.VMEM((2, chunk // 2, 128), F32),
            pltpu.VMEM((2, chunk, 128), F32),
            pltpu.VMEM((n_y, 24, 128), F32),
            pltpu.VMEM((n_y, 24, 128), F32),
            pltpu.VMEM((n_z, 4 * y_lo, 128), F32),
            pltpu.VMEM((n_z, 4 * y_lo, 128), F32),
            pltpu.VMEM((n_z, 4 * y_lo, 128), F32),
            pltpu.VMEM((n_z, 4 * y_lo, 128), F32),
            pltpu.VMEM((y_lo, 24, 128), F32),
            pltpu.VMEM((24, FINE, width), F32),
            pltpu.VMEM(outer_high.shape, BF16),
            pltpu.VMEM(outer_low.shape, BF16),
            pltpu.VMEM(back_high.shape, BF16),
            pltpu.VMEM(back_low.shape, BF16),
            pltpu.SemaphoreType.DMA((n_sem,)),
            pltpu.SemaphoreType.DMA((n_sem,)),
            pltpu.SemaphoreType.DMA((4,)),
        ],
        compiler_params=pltpu.CompilerParams(
            collective_id=0, has_side_effects=True, vmem_limit_bytes=50 * 1024 * 1024
        ),
    )(
        spectra, ids, weights, block_live, windows, observed,
        jnp.asarray(outer_high), jnp.asarray(outer_low), jnp.asarray(back_high), jnp.asarray(back_low),
        jnp.asarray(inner), jnp.asarray(inner_back), jnp.asarray(twiddle),
    )


def solution(mesh, y_lo=None):
    n_pair = mesh.shape["pair"]
    y_lo = y_lo or max(1, n_pair // 8)
    in_specs = (
        P("day", None, "pair", None),
        P(),
        P(),
        P(("pair", "day")),
        P(("pair", "day"), None, None),
        P(("pair", "day"), None, None),
    )
    out_specs = P("day", None, "pair", None)
    return jax.shard_map(
        functools.partial(body, y_lo, n_pair // y_lo), mesh=mesh, in_specs=in_specs, out_specs=out_specs, check_vma=False
    )
```

time: 497 us -> 69.3 us (0.14)
  waiting for transfers between devices: 207 us -> 0 us
  other arithmetic: 148 us -> 0 us
  Pallas kernels: 0 us -> 57.3 us
  matrix products: 45 us -> 0 us
  blocking collectives: 39.5 us -> 0 us
  local copies, waits for them, and re-layouts: 29.9 us -> 10.9 us
  between operations: 14.4 us -> 0.81 us
  starting transfers between devices: 11.5 us -> 0 us
    psum x1 -> x0, waiting for transfers between devices: 189 us -> none  [body(): total = lax.psum(local_stack, 'day')]
    another operation x18 -> x0, other arithmetic: 141 us -> none
    pallas_call x0 -> x1, Pallas kernels: none -> 57.3 us  [body(): pl.pallas_call(functools.partial(kernel, (y_lo, n_z), 32), out_shape=jax....]
    dot_general x25 -> x0, matrix products: 45 us -> none  [the longest x16 35.5 us: lag_step(): lax.dot_general(misfit, block_table, (((1,), (1,)), ((), ())), preferred_...]
    all_gather x1 -> x0, blocking collectives: 39.5 us -> none  [body(): all_pairs = lax.all_gather(spread, 'day', axis=1, tiled=True)]
    all_to_all x2 -> x0, waiting for transfers between devices: 18.2 us -> none  [the longest x1 9.09 us: body(): lax.all_to_all(adjoint_split, 'pair', split_axis=2, concat_axis=1, tiled=...]
    all_to_all x2 -> x0, starting transfers between devices: 11.5 us -> none  [the longest x1 7.66 us: body(): lax.all_to_all(day_share, 'pair', split_axis=1, concat_axis=2, tiled=True)]
    unnamed x29 -> x20, local copies, waits for them, and re-layouts: 10.3 us -> 2.94 us
  transfers between devices with their start and end apart: 3 -> 0, of which waited for: 3 -> 0; matrix products, arithmetic and copies ran while one was open for 0% -> 0% of each run, Pallas kernels for 0% -> 0%
where the time goes in v1:
time: 69.3 us; the launch traced here: 69 us
  Pallas kernels  57.3 us (83%)
  local copies, waits for them, and re-layouts  10.9 us (16%)
  between operations  0.81 us (1%)
    pallas_call x1, Pallas kernels, body(): pl.pallas_call(functools.partial(kernel, (y_lo, n_z), 32), out_shape=jax....  57.3 us
    transpose x1, local copies, waits for them, and re-layouts, body(): pair_stations.reshape(y_lo, n_z, 2, 4, 2, 3, 2)  4.25 us
    unnamed x20, local copies, waits for them, and re-layouts  2.94 us
    reshape x1, local copies, waits for them, and re-layouts, body(): pair_stations.reshape(y_lo, n_z, 2, 4, 2, 3, 2)  1.55 us

profile of v1, /device:TPU:1, one launch (start us, length us, event | category | flops | bytes accessed | tf_op | source)
XLA Modules:
  0.0 69.0 jit_solution(15880461192402711382)
XLA Ops:
  0.0 1.1 %reshape.11 = f32[8,4,8,2,32]{4,3,2,1,0:T(2,128)S(1)} reshape(f32[8,2048]{1,0:T(8,128)} %param.14) | data formatting | bytes 131072 | tf_op jit(solution)/shard_map/reshape | solution.py:372
  1.1 0.1 copy.18
  1.2 0.3 broadcast_in_dim.2
  1.5 0.6 reshape.12
  2.0 0.0 copy-start.7
  2.1 0.0 copy-start.2
  2.1 0.2 copy.19.weights
  2.3 0.5 copy-done.7
  2.8 0.0 copy-start.1
  2.8 1.6 %reshape.10 = s32[4,8,2,4,2,3,2]{5,4,3,2,1,0,6:T(2,128)} reshape(s32[1536,2]{0,1:T(2,128)S(1)} %copy-done.7) | data formatting | bytes 24576 | tf_op jit(solution)/shard_map/reshape | solution.py:367
  4.3 0.0 copy-start
  4.3 0.0 copy-start.5
  4.3 4.2 %copy.17 = s32[2,4,2,4,3,8,2]{6,5,4,3,2,1,0:T(8,128)S(1)} copy(s32[2,4,2,4,3,8,2]{4,0,1,2,5,3,6:T(2,128)} %bitcast.8) | data formatting | bytes 24576 | tf_op jit(solution)/shard_map/transpose | solution.py:367
  8.6 0.0 copy-done.8
  8.6 0.1 copy.20.windows
  9.4 0.0 copy-done.2
  9.4 0.0 copy-done.1
  9.4 0.0 copy-done
  9.4 0.0 copy-done.3
  9.4 0.0 copy-done.4
  9.4 0.0 copy-done.5
  9.4 0.0 copy-done.6
  9.4 57.3 %shard_map.127 = f32[2,2,64,1024]{3,2,1,0:T(8,128)} custom-call(bf16[2,2,64,1024]{3,2,1,0:T(8,128)(2,1)S(1)} %copy-done.2, s32[8,192,2]{2,1,0:T(8,128)S(1)} %bitcast.7, f32[8,64,128]{2,1,0:T(8,128)S(1)} %copy.19.weights, s32[1]{0:T(128)S(6)} %copy.22.live, s32[3,8,2]{2,1,0:T(8,128)S(1)} %copy.20.windows, bf16[3,8,4096]{2,1,0:T(8,128)(2,1)S(1)} %copy-done.3, ...), custom_call_target="tpu_custom_call" | custom-call | tf_op jit(solution)/shard_map/pallas_call | solution.py:379
  66.7 2.3 %copy.23 = f32[2,2,64,1024]{3,2,1,0:T(8,128)} copy(f32[2,2,64,1024]{3,2,1,0:T(8,128)} %shard_map.127) | data formatting | bytes 2097152
  (4 shorter events, 0.0 us)
Async XLA Ops:
  2.0 0.7 %copy-start.7 = (s32[1536,2]{0,1:T(2,128)S(1)}, s32[1536,2]{0,1:T(2,128)}, u32[]{:S(2)}) copy-start(s32[1536,2]{0,1:T(2,128)} %param.15) | copy-start | bytes 36868
  2.1 7.3 %copy-start.2 = (bf16[2,2,64,1024]{3,2,1,0:T(8,128)(2,1)S(1)}, bf16[2,2,64,1024]{3,2,1,0:T(8,128)(2,1)}, u32[]{:S(2)}) copy-start(bf16[2,2,64,1024]{3,2,1,0:T(8,128)(2,1)} %spec.1) | copy-start | bytes 1572868
  2.8 6.6 %copy-start.1 = (bf16[512,768]{1,0:T(8,128)(2,1)S(1)}, bf16[512,768]{1,0:T(8,128)(2,1)}, u32[]{:S(2)}) copy-start(bf16[512,768]{1,0:T(8,128)(2,1)} %constant.15.clone.outer_low_hbm) | copy-start | bytes 2359300
  4.3 5.1 %copy-start = (bf16[512,768]{1,0:T(8,128)(2,1)S(1)}, bf16[512,768]{1,0:T(8,128)(2,1)}, u32[]{:S(2)}) copy-start(bf16[512,768]{1,0:T(8,128)(2,1)} %constant.14.clone.outer_high_hbm) | copy-start | bytes 2359300
  4.3 4.3 %copy-start.8 = (s32[3,8,2]{1,2,0:T(2,128)S(1)}, s32[3,8,2]{1,2,0:T(2,128)}, u32[]{:S(2)}) copy-start(s32[3,8,2]{1,2,0:T(2,128)} %param.17) | copy-start | bytes 580
  4.3 5.1 %copy-start.3 = (bf16[3,8,4096]{2,1,0:T(8,128)(2,1)S(1)}, bf16[3,8,4096]{2,1,0:T(8,128)(2,1)}, u32[]{:S(2)}) copy-start(bf16[3,8,4096]{2,1,0:T(8,128)(2,1)} %observed.1) | copy-start | bytes 589828
  4.3 5.1 %copy-start.4 = (bf16[128,32]{1,0:T(8,128)(2,1)S(1)}, bf16[128,32]{1,0:T(8,128)(2,1)}, u32[]{:S(2)}) copy-start(bf16[128,32]{1,0:T(8,128)(2,1)} %constant.19.clone.inner_back) | copy-start | bytes 24580
  4.3 5.1 %copy-start.5 = (f32[2,32,128]{2,1,0:T(8,128)S(1)}, f32[2,32,128]{2,1,0:T(8,128)}, u32[]{:S(2)}) copy-start(f32[2,32,128]{2,1,0:T(8,128)} %constant.20.clone.twiddle) | copy-start | bytes 98308
  8.6 0.8 %copy-start.6 = (bf16[64,64]{1,0:T(8,128)(2,1)S(1)}, bf16[64,64]{1,0:T(8,128)(2,1)}, u32[]{:S(2)}) copy-start(bf16[64,64]{1,0:T(8,128)(2,1)} %constant.18.clone.inner) | copy-start | bytes 24580
